TPU v7x, 512 devices: a whole 4x8x8 slice. The times are simulated.
512 devices in a mesh: grid: 64 (over x, y, core), layer: 8 (over z).
Axes of the slice: x: 4, y: 8, z: 8, core: 2. Of those that a mesh axis runs over, the one named last changes fastest.
Arguments:
- tensor_blocks: bfloat16 [32768, 64, 128], P(('grid', 'layer')), may hold values from -6 to 6
- tensor_screen: int32 [512, 2], P(('grid', 'layer')), may hold values 0 or 1
- density: bfloat16 [32768, 512], P(('grid', 'layer')), may hold values from -0.03125 to 0.03125
- density_screen: int32 [512, 8], P(('grid', 'layer')), may hold values 0 or 1
Outputs:
- contracted: bfloat16 [512, 64, 128], P(('grid', 'layer'))
Inputs may be any that keep to these rules, and one draw needn't show every extreme that they name: `tensor_screen`: 1 where the pair of atom blocks survives screening, else 0. `density_screen`: 1 where the pair of atom blocks survives screening, else 0.
All inputs are finite; a program needn't handle non-finite values.
Results may differ from a plain program's by a relative error of at most 0.0022.
Values may be sent and summed in bfloat16 or wider, within the bound.
A program may use at most 64 MiB of HBM per device.

v0:
```python
import jax
import jax.numpy as jnp
from jax import lax
from jax.sharding import PartitionSpec as P


def body(tensor_blocks, tensor_screen, density, density_screen):
    block_fns = tensor_blocks.shape[0]
    aux_all = tensor_blocks.shape[1]
    orbital_all = tensor_blocks.shape[2]
    orbital_blocks = tensor_screen.shape[1]
    grid_count = lax.axis_size("grid")
    layer_count = lax.axis_size("layer")
    tensor_mask = tensor_screen[0].astype(jnp.bfloat16)
    screened = (
        tensor_blocks.reshape(block_fns, aux_all, orbital_blocks, block_fns)
        * tensor_mask[None, None, :, None]
    )
    screened = screened.reshape(block_fns, aux_all, orbital_all)
    col_blocks = density_screen.shape[1]
    col_width = density.shape[1]
    density_mask = density_screen[0].astype(jnp.bfloat16)
    kept_density = density.reshape(block_fns, col_blocks, block_fns) * density_mask[None, :, None]
    kept_density = kept_density.reshape(block_fns, col_width)
    per_device = col_width // (grid_count * layer_count)
    regrouped = lax.all_to_all(screened, "grid", split_axis=1, concat_axis=0, tiled=True)
    aux_local = regrouped.shape[1]
    flat_rows = aux_local * orbital_all
    operand = regrouped.reshape(regrouped.shape[0], flat_rows)
    update = lax.dot_general(
        lax.all_gather(kept_density, "grid", axis=0, tiled=True),
        operand,
        (((0,), (0,)), ((), ())),
        preferred_element_type=jnp.float32,
    )
    arranged = update.reshape(grid_count, layer_count * per_device, aux_local, orbital_all)
    remapped = lax.all_to_all(arranged, "grid", split_axis=0, concat_axis=2, tiled=True)
    layer_terms = remapped.reshape(layer_count, per_device, aux_local * grid_count, orbital_all)
    reduced = lax.psum_scatter(layer_terms, "layer", scatter_dimension=0, tiled=True)
    return reduced.reshape(per_device, aux_local * grid_count, orbital_all).astype(jnp.bfloat16)


def solution(mesh):
    in_specs = (
        P(("grid", "layer"), None, None),
        P(("grid", "layer"), None),
        P(("grid", "layer"), None),
        P(("grid", "layer"), None),
    )
    out_specs = P(("grid", "layer"), None, None)
    return jax.shard_map(body, mesh=mesh, in_specs=in_specs, out_specs=out_specs, check_vma=False)
```

profile of v0, /device:TPU:6, one launch (start us, length us, event | category | flops | bytes accessed | tf_op | source)
XLA Modules:
  0.0 176.3 jit_solution(14379365550426218398)
XLA Ops:
  6.5 0.0 all-gather.2.cloned.1.call-start
  6.5 0.7 convert_bitcast_fusion.2
  7.2 0.1 mul.26
  7.3 0.1 mul.27
  7.4 1.5 broadcast_multiply_fusion
  8.8 0.0 all-gather.2.cloned.1.call-update
  8.8 0.7 convert_bitcast_fusion.1
  9.5 0.1 mul.30
  9.6 0.1 mul.31
  9.7 2.9 %copy_multiply_fusion = bf16[64,64,128]{2,0,1:T(8,128)(2,1)} fusion(bf16[64,64,128]{2,1,0:T(8,128)(2,1)} %param.4, bf16[128]{0:T(256)(128)(2,1)S(1)} %mul.31), kind=kLoop, calls=%fused_computation.3 | loop fusion | flops 524288 | bytes 2097408 | tf_op jit(solution)/shard_map/mul | solution.py:16
  12.6 10.8 %all-to-all-start = ((bf16[64,64,128]{2,0,1:T(8,128)(2,1)}), bf16[64,64,128]{2,0,1:T(8,128)(2,1)S(1)}, u32[]{:S(2)}, u32[]{:S(2)}) async-start(bf16[64,64,128]{2,0,1:T(8,128)(2,1)} %copy_multiply_fusion), calls=%async_computation | async-start | bytes 2097152 | tf_op jit(solution)/shard_map/all_to_all | solution.py:26
  23.4 0.0 reduce-scatter.2.cloned.1.call-start
  23.5 76.8 %all-gather.2.cloned.1.call-done = bf16[4096,512]{1,0:T(8,128)(2,1)} async-done(((bf16[64,512]{1,0:T(8,128)(2,1)}), bf16[4096,512]{1,0:T(8,128)(2,1)}) %all-gather.2.cloned.1.call-update) | async-done | bytes 4194320 | tf_op jit(solution)/shard_map/all_gather | solution.py:31
  100.2 6.4 %copy.9 = bf16[512,4096]{1,0:T(8,128)(2,1)} copy(bf16[512,4096]{0,1:T(8,128)(2,1)} %bitcast.29) | data formatting | bytes 8388608 | tf_op jit(solution)/shard_map/dot_general | solution.py:30
  106.6 0.0 all-to-all-done
  106.6 3.4 %fusion.2 = f32[64,8,1,128]{3,1,2,0:T(8,128)S(1)} fusion(bf16[4096,128,1]{1,0,2:T(8,128)(2,1)S(1)} %bitcast.30, bf16[512,4096]{1,0:T(8,128)(2,1)} %copy.9), kind=kOutput, calls=%fused_computation.2 | convolution fusion | flops 536870912 | bytes 5505024 | tf_op jit(solution)/shard_map/dot_general | solution.py:30
  110.0 19.6 %all_to_all.30 = f32[64,8,1,128]{3,1,2,0:T(8,128)S(1)} all-to-all(f32[64,8,1,128]{3,1,2,0:T(8,128)S(1)} %fusion.2), channel_id=1, replica_groups=mesh['grid'=64,'layer'=8] {'grid'}, dimensions={0} | all-to-all | bytes 524288 | tf_op jit(solution)/shard_map/all_to_all | solution.py:37
  129.7 0.7 copy.12
  130.4 0.0 reduce-scatter.2.cloned.1.call-update
  130.5 37.6 %reduce-scatter.2.cloned.1.call-done = f32[1,1,64,128]{3,2,1,0:T(8,128)} async-done(((f32[8,1,64,128]{3,2,1,0:T(8,128)}), f32[1,1,64,128]{3,2,1,0:T(8,128)}) %reduce-scatter.2.cloned.1.call-update) | async-done | bytes 32784 | tf_op jit(solution)/shard_map/reduce_scatter | solution.py:39
  168.1 1.4 convert_bitcast_fusion
Async XLA Ops:
  6.5 93.7 %all-gather.2.cloned.1.call-start = ((), (), s32[]{:S(2)}) async-start(), calls=%async_computation.3 | async-start | bytes 4259840 | tf_op jit(solution)/shard_map/all_gather | solution.py:31
  12.6 94.0 %all-to-all-start = ((bf16[64,64,128]{2,0,1:T(8,128)(2,1)}), bf16[64,64,128]{2,0,1:T(8,128)(2,1)S(1)}, u32[]{:S(2)}, u32[]{:S(2)}) async-start(bf16[64,64,128]{2,0,1:T(8,128)(2,1)} %copy_multiply_fusion), calls=%async_computation | async-start | bytes 2097152 | tf_op jit(solution)/shard_map/all_to_all | solution.py:26
  23.4 144.7 %reduce-scatter.2.cloned.1.call-start = ((), (), s32[]{:S(2)}) async-start(), calls=%async_computation.4 | async-start | bytes 294912 | tf_op jit(solution)/shard_map/reduce_scatter | solution.py:39
Sparse Core Ops, SparseCore 0:
  10.7 89.4 all-gather.1
  130.6 37.4 reduce-scatter.1
where the time goes:
time: 177 us; the launch traced here: 176 us
  waiting for transfers between devices  114 us (64%)
  blocking collectives  19.6 us (11%)
  between operations  13.4 us (8%)
  starting transfers between devices  10.8 us (6%)
  local copies, waits for them, and re-layouts  7.43 us (4%)
  other arithmetic  7.07 us (4%)
  matrix products  3.44 us (2%)
    all_gather x1, waiting for transfers between devices, body(): lax.all_gather(kept_density, 'grid', axis=0, tiled=True)  76.8 us
    reduce_scatter x1, waiting for transfers between devices, body(): lax.psum_scatter(layer_terms, 'layer', scatter_dimension=0, tiled=True)  37.6 us
    all_to_all x1, blocking collectives, body(): lax.all_to_all(arranged, 'grid', split_axis=0, concat_axis=2, tiled=True)  19.6 us
    all_to_all x1, starting transfers between devices, body(): lax.all_to_all(screened, 'grid', split_axis=1, concat_axis=0, tiled=True)  10.8 us
    dot_general x1, local copies, waits for them, and re-layouts, body(): lax.dot_general(lax.all_gather(kept_density, 'grid', axis=0, tiled=True),...  6.36 us
  transfers between devices with their start and end apart: 3, of which 2 were waited for; matrix products, arithmetic and copies ran while one was open for 6% of the time, Pallas kernels for 0%

commit v1 on v0

v1 whole, which is shorter than its diff:
```python
import functools

import jax
import jax.numpy as jnp
from jax import lax
from jax.experimental import pallas as pl
from jax.experimental.pallas import tpu as pltpu
from jax.sharding import PartitionSpec as P

MESH = pl.DeviceIdType.MESH

NX, RING, CORES = 4, 8, 2
GROUP = NX * CORES
ROWS = 64
NAUX = 64
LANES = 128
NSIG = 512
CHUNKS = 4
PAIR = 2 * LANES
DEPTH = GROUP * ROWS
SLAB = GROUP * RING


def remote(src, dst, send_sem, recv_sem, device):
    return pltpu.make_async_remote_copy(
        src_ref=src, dst_ref=dst, send_sem=send_sem, recv_sem=recv_sem,
        device_id=device, device_id_type=MESH)


def kernel(tensor_hbm, tscreen, density_hbm, dscreen, out_ref,
           tb, tf, stage, recv_t, db, dall, perm, dt, part, near, mid, tie, far,
           first, recv_b, tiles, outgoing, fin,
           load_sem, own_sem, d_send, d_recv, t_send, t_recv,
           near_send, near_recv, mid_send, mid_recv, tie_send, tie_recv, far_send, far_recv,
           b_send, b_recv, f_send, f_recv):
    grid = lax.axis_index("grid")
    z = lax.axis_index("layer")
    core = lax.rem(grid, CORES)
    y = lax.rem(grid // CORES, RING)
    x = grid // (CORES * RING)
    me = x * CORES + core

    def at(x_, y_, core_, z_):
        return ((x_ * RING + y_) * CORES + core_, z_)

    def member(pos):
        return at(pos // CORES, y, lax.rem(pos, CORES), z)

    a = jnp.where(core == 0, y, z)
    b = jnp.where(core == 0, z, y)

    def on_a(i):
        return at(x, jnp.where(core == 0, i, y), core, jnp.where(core == 0, z, i))

    def on_b(i):
        return at(x, jnp.where(core == 0, y, i), core, jnp.where(core == 0, i, z))

    def ring(i):
        return lax.rem(i + 2 * RING, RING)

    load_t = pltpu.make_async_copy(tensor_hbm, tb, load_sem.at[0])
    load_d = pltpu.make_async_copy(density_hbm, db, load_sem.at[1])
    load_d.start()
    load_t.start()

    barrier = pltpu.get_barrier_semaphore()
    peers = [member(lax.rem(me + d, GROUP)) for d in range(1, GROUP)]
    peers += [on_a(ring(a + d)) for d in (1, 2, -1, -2)]
    peers += [on_b(ring(b + d)) for d in range(1, RING)]
    for peer in peers:
        pl.semaphore_signal(barrier, inc=1, device_id=peer, device_id_type=MESH)

    my_rows = pl.ds(pl.multiple_of(me * ROWS, ROWS), ROWS)
    lane = lax.broadcasted_iota(jnp.int32, (ROWS, LANES), 1)
    load_d.wait()
    for t in range(NSIG // LANES):
        cols = pl.ds(t * LANES, LANES)
        low = dscreen[0, 2 * t].astype(jnp.float32)
        high = dscreen[0, 2 * t + 1].astype(jnp.float32)
        keep = jnp.where(lane < 64, low, high)
        dall[my_rows, cols] = (db[:, cols].astype(jnp.float32) * keep).astype(jnp.bfloat16)

    keep_t = jnp.where(lane < 64, tscreen[0, 0].astype(jnp.float32), tscreen[0, 1].astype(jnp.float32))
    load_t.wait()

    @pl.loop(0, ROWS, unroll=8)
    def _(n):
        tf[pl.ds(pl.multiple_of(n * NAUX, NAUX), NAUX), :] = tb[n].astype(jnp.float32) * keep_t

    def regroup(c):
        for pos in range(GROUP):
            for h in range(2):
                p = pos * 8 + 2 * c + h
                rows = tf[pl.ds(p, ROWS, stride=NAUX), :]
                stage[c, pos, :, h * LANES:(h + 1) * LANES] = rows.astype(jnp.bfloat16)

    regroup(0)
    pl.semaphore_wait(barrier, len(peers))

    other = at(x, y, 1 - core, z)
    d_copies = []
    for d in range(1, NX):
        peer = at(lax.rem(x + d, NX), y, core, z)
        d_copies.append(remote(dall.at[my_rows], dall.at[my_rows], d_send.at[d - 1], d_recv.at[d - 1], peer))
    d_copies.append(remote(dall.at[my_rows], dall.at[my_rows], d_send.at[3], d_recv.at[3], other))
    for copy in d_copies:
        copy.start()

    t_copies = {}

    def send_t(c):
        for d in range(1, GROUP):
            pos = lax.rem(me + d, GROUP)
            copy = remote(stage.at[c, pos], recv_t.at[c, my_rows], t_send.at[c, d - 1], t_recv.at[c, d - 1],
                          member(pos))
            copy.start()
            t_copies[c, d] = copy
        own = pltpu.make_async_copy(stage.at[c, me], recv_t.at[c, my_rows], own_sem.at[c])
        own.start()
        t_copies[c, 0] = own

    send_t(0)
    for c in range(1, CHUNKS):
        regroup(c)
        send_t(c)

    row = lax.broadcasted_iota(jnp.int32, (SLAB, NSIG), 0)
    col = lax.broadcasted_iota(jnp.int32, (SLAB, NSIG), 1)
    j = row & 7
    for block in range(RING):
        y_ = jnp.where(core == 0, block, row >> 3)
        z_ = jnp.where(core == 0, row >> 3, block)
        sigma = (j >> 1) * 128 + y_ * 16 + (j & 1) * 8 + z_
        perm[block * SLAB:(block + 1) * SLAB, :] = jnp.where(sigma == col, 1.0, 0.0).astype(jnp.bfloat16)

    relays = []
    for d in range(1, NX):
        d_copies[d - 1].wait_recv()
        src = lax.rem(x + NX - d, NX) * CORES + core
        rows = pl.ds(pl.multiple_of(src * ROWS, ROWS), ROWS)
        copy = remote(dall.at[rows], dall.at[rows], d_send.at[3 + d], d_recv.at[3 + d], other)
        copy.start()
        relays.append(copy)
    d_copies[3].wait_recv()
    for copy in relays:
        copy.wait_recv()
    dt[...] = lax.dot_general(perm[...], dall[...], (((1,), (1,)), ((), ())),
                              preferred_element_type=jnp.float32).astype(jnp.bfloat16)

    def slab(c, i):
        return part.at[c, pl.ds(pl.multiple_of(ring(i) * SLAB, SLAB), SLAB)]

    started = []

    def go(copy):
        copy.start()
        started.append(copy)
        return copy

    near_c, mid_c, tie_c, far_c, b_c = {}, {}, {}, {}, {}

    def multiply(c):
        t_copies[c, 0].wait()
        for d in range(1, GROUP):
            t_copies[c, d].wait_recv()
        part[c] = jnp.dot(dt[...], recv_t[c], preferred_element_type=jnp.float32)
        for k, step in enumerate((1, -1)):
            to = on_a(ring(a + step))
            mid_c[c, k] = go(remote(slab(c, a + 3 * step), mid.at[c, k], mid_send.at[c, k], mid_recv.at[c, k], to))
        step = -2 if c % 2 == 0 else 2
        tie_c[c] = go(remote(slab(c, a + 4), tie.at[c], tie_send.at[c], tie_recv.at[c], on_a(ring(a + step))))
        for k, step in enumerate((1, -1)):
            to = on_a(ring(a + step))
            near_c[c, k] = go(remote(slab(c, a + step), near.at[c, k], near_send.at[c, k], near_recv.at[c, k], to))

    def forward(c):
        for k, step in enumerate((2, -2)):
            mid_c[c, k].wait_recv()
            with_tie = k == (1 if c % 2 == 0 else 0)
            if with_tie:
                tie_c[c].wait_recv()
            mine = slab(c, a + step)
            total = mine[...] + mid[c, k]
            if with_tie:
                total = total + tie[c]
            mine[...] = total
            far_c[c, k] = go(remote(mine, far.at[c, k], far_send.at[c, k], far_recv.at[c, k],
                                    on_a(ring(a + step))))

    def reduce_a(c):
        for k in range(2):
            near_c[c, k].wait_recv()
            far_c[c, k].wait_recv()
        first[c] = (slab(c, a)[...] + near[c, 0]) + near[c, 1] + (far[c, 0] + far[c, 1])
        for d in range(1, RING):
            to = ring(b + d)
            rows = pl.ds(pl.multiple_of(to * GROUP, GROUP), GROUP)
            b_c[c, d] = go(remote(first.at[c, rows], recv_b.at[c, d - 1], b_send.at[c, d - 1],
                                  b_recv.at[c, d - 1], on_b(to)))

    def reduce_b(c):
        rows = pl.ds(pl.multiple_of(b * GROUP, GROUP), GROUP)
        total = first[c, rows, :]
        for d in range(1, RING):
            b_c[c, d].wait_recv()
            total = total + recv_b[c, d - 1]
        for h in range(2):
            p = 2 * c + h
            tiles[p * GROUP:(p + 1) * GROUP, :] = total[:, h * LANES:(h + 1) * LANES]

    multiply(0)
    multiply(1)
    forward(0)
    multiply(2)
    forward(1)
    reduce_a(0)
    multiply(3)
    forward(2)
    reduce_a(1)
    forward(3)
    reduce_a(2)
    reduce_b(0)
    reduce_a(3)
    for c in range(1, CHUNKS):
        reduce_b(c)

    for k in range(GROUP):
        outgoing[k] = tiles[pl.ds(k, 8, stride=GROUP), :]
    my_p = pl.ds(pl.multiple_of(me * 8, 8), 8)
    f_c = []
    for d in range(1, GROUP):
        pos = lax.rem(me + d, GROUP)
        f_c.append(go(remote(outgoing.at[pos], fin.at[my_p], f_send.at[d - 1], f_recv.at[d - 1], member(pos))))
    fin[my_p, :] = outgoing[me]
    for copy in f_c:
        copy.wait_recv()
    out_ref[...] = fin[...].astype(jnp.bfloat16)

    for copy in d_copies + relays + started:
        copy.wait_send()
    for c in range(CHUNKS):
        for d in range(1, GROUP):
            t_copies[c, d].wait_send()


def body(tensor_blocks, tensor_screen, density, density_screen):
    dma = pltpu.SemaphoreType.DMA
    out = pl.pallas_call(
        kernel,
        out_shape=jax.ShapeDtypeStruct((NAUX, LANES), jnp.bfloat16),
        in_specs=[
            pl.BlockSpec(memory_space=pl.ANY),
            pl.BlockSpec(memory_space=pltpu.SMEM),
            pl.BlockSpec(memory_space=pl.ANY),
            pl.BlockSpec(memory_space=pltpu.SMEM),
        ],
        out_specs=pl.BlockSpec(memory_space=pltpu.VMEM),
        scratch_shapes=[
            pltpu.VMEM((ROWS, NAUX, LANES), jnp.bfloat16),
            pltpu.VMEM((ROWS * NAUX, LANES), jnp.float32),
            pltpu.VMEM((CHUNKS, GROUP, ROWS, PAIR), jnp.bfloat16),
            pltpu.VMEM((CHUNKS, DEPTH, PAIR), jnp.bfloat16),
            pltpu.VMEM((ROWS, NSIG), jnp.bfloat16),
            pltpu.VMEM((DEPTH, NSIG), jnp.bfloat16),
            pltpu.VMEM((NSIG, NSIG), jnp.bfloat16),
            pltpu.VMEM((NSIG, DEPTH), jnp.bfloat16),
            pltpu.VMEM((CHUNKS, NSIG, PAIR), jnp.float32),
            pltpu.VMEM((CHUNKS, 2, SLAB, PAIR), jnp.float32),
            pltpu.VMEM((CHUNKS, 2, SLAB, PAIR), jnp.float32),
            pltpu.VMEM((CHUNKS, SLAB, PAIR), jnp.float32),
            pltpu.VMEM((CHUNKS, 2, SLAB, PAIR), jnp.float32),
            pltpu.VMEM((CHUNKS, SLAB, PAIR), jnp.float32),
            pltpu.VMEM((CHUNKS, RING - 1, GROUP, PAIR), jnp.float32),
            pltpu.VMEM((8 * GROUP, LANES), jnp.float32),
            pltpu.VMEM((GROUP, 8, LANES), jnp.float32),
            pltpu.VMEM((NAUX, LANES), jnp.float32),
            dma((2,)), dma((CHUNKS,)),
            dma((7,)), dma((7,)),
            dma((CHUNKS, 7)), dma((CHUNKS, 7)),
            dma((CHUNKS, 2)), dma((CHUNKS, 2)),
            dma((CHUNKS, 2)), dma((CHUNKS, 2)),
            dma((CHUNKS,)), dma((CHUNKS,)),
            dma((CHUNKS, 2)), dma((CHUNKS, 2)),
            dma((CHUNKS, 7)), dma((CHUNKS, 7)),
            dma((7,)), dma((7,)),
        ],
        compiler_params=pltpu.CompilerParams(
            collective_id=0, has_side_effects=True, vmem_limit_bytes=40 << 20),
        name="contract",
    )(tensor_blocks, tensor_screen, density, density_screen)
    return out.reshape(1, NAUX, LANES)


def solution(mesh):
    in_specs = (
        P(("grid", "layer"), None, None),
        P(("grid", "layer"), None),
        P(("grid", "layer"), None),
        P(("grid", "layer"), None),
    )
    out_specs = P(("grid", "layer"), None, None)
    return jax.shard_map(body, mesh=mesh, in_specs=in_specs, out_specs=out_specs, check_vma=False)
```

time: 177 us -> 59.5 us (0.34)
  the two profiles are of different devices: /device:TPU:6 before, /device:TPU:1 now
where the time goes in v1:
time: 59.5 us; the launch traced here: 59.3 us
  Pallas kernels  55.3 us (93%)
  local copies, waits for them, and re-layouts  3.98 us (7%)
    pallas_call x1, Pallas kernels, body(): pl.pallas_call(kernel, out_shape=jax.ShapeDtypeStruct((NAUX, LANES), jnp....  55.3 us
    unnamed x9, local copies, waits for them, and re-layouts  3.98 us

profile of v1, /device:TPU:1, one launch (start us, length us, event | category | flops | bytes accessed | tf_op | source)
XLA Modules:
  0.0 59.3 jit_solution(11043692064951641479)
XLA Ops:
  0.0 0.0 copy-start
  0.0 1.2 %copy-done = bf16[64,64,128]{2,1,0:T(8,128)(2,1)S(1)} copy-done((bf16[64,64,128]{2,1,0:T(8,128)(2,1)S(1)}, bf16[64,64,128]{2,1,0:T(8,128)(2,1)}, u32[]{:S(2)}) %copy-start) | copy-done | bytes 1048600
  1.2 0.0 copy-start.1
  1.2 0.8 %copy-done.1 = bf16[64,512]{1,0:T(8,128)(2,1)S(1)} copy-done((bf16[64,512]{1,0:T(8,128)(2,1)S(1)}, bf16[64,512]{1,0:T(8,128)(2,1)}, u32[]{:S(2)}) %copy-start.1) | copy-done | bytes 65560
  2.1 0.0 copy-start.2
  2.1 0.7 %copy-done.2 = s32[1,2]{1,0:T(1,128)S(1)} copy-done((s32[1,2]{1,0:T(1,128)S(1)}, s32[1,2]{1,0:T(1,128)}, u32[]{:S(2)}) %copy-start.2) | copy-done | bytes 32
  2.7 0.0 copy-start.3
  2.7 0.7 %copy-done.3 = s32[1,8]{1,0:T(1,128)S(1)} copy-done((s32[1,8]{1,0:T(1,128)S(1)}, s32[1,8]{1,0:T(1,128)}, u32[]{:S(2)}) %copy-start.3) | copy-done | bytes 56
  3.4 55.3 %contract.1 = bf16[64,128]{1,0:T(8,128)(2,1)S(1)} custom-call(bf16[64,64,128]{2,1,0:T(8,128)(2,1)S(1)} %copy-done, s32[1,2]{1,0:T(1,128)S(1)} %copy-done.2, bf16[64,512]{1,0:T(8,128)(2,1)S(1)} %copy-done.1, s32[1,8]{1,0:T(1,128)S(1)} %copy-done.3), custom_call_target="tpu_custom_call" | custom-call | tf_op jit(solution)/shard_map/contract/pallas_call | solution.py:248
  58.7 0.6 %copy.6 = bf16[1,64,128]{2,1,0:T(8,128)(2,1)} copy(bf16[1,64,128]{2,1,0:T(8,128)(2,1)S(1)} %bitcast.1) | data formatting | bytes 32768
Async XLA Ops:
  0.0 1.2 %copy-start = (bf16[64,64,128]{2,1,0:T(8,128)(2,1)S(1)}, bf16[64,64,128]{2,1,0:T(8,128)(2,1)}, u32[]{:S(2)}) copy-start(bf16[64,64,128]{2,1,0:T(8,128)(2,1)} %tensor_hbm.1) | copy-start | bytes 3145732
  1.2 0.8 %copy-start.1 = (bf16[64,512]{1,0:T(8,128)(2,1)S(1)}, bf16[64,512]{1,0:T(8,128)(2,1)}, u32[]{:S(2)}) copy-start(bf16[64,512]{1,0:T(8,128)(2,1)} %density_hbm.1) | copy-start | bytes 196612
  2.1 0.7 %copy-start.2 = (s32[1,2]{1,0:T(1,128)S(1)}, s32[1,2]{1,0:T(1,128)}, u32[]{:S(2)}) copy-start(s32[1,2]{1,0:T(1,128)} %tscreen.1) | copy-start | bytes 28
  2.7 0.7 %copy-start.3 = (s32[1,8]{1,0:T(1,128)S(1)}, s32[1,8]{1,0:T(1,128)}, u32[]{:S(2)}) copy-start(s32[1,8]{1,0:T(1,128)} %dscreen.1) | copy-start | bytes 100

commit v2 on v1

v2 whole, which is shorter than its diff:
```python
import jax
import jax.numpy as jnp
from jax import lax
from jax.experimental import pallas as pl
from jax.experimental.pallas import tpu as pltpu
from jax.sharding import PartitionSpec as P

MESH = pl.DeviceIdType.MESH

NX, RING, CORES = 4, 8, 2
GROUP = NX * CORES
ROWS = 64
NAUX = 64
LANES = 128
NSIG = 512
SLICES = 4
WIDE = NAUX // SLICES
SHARE = NAUX // GROUP * LANES
PARTS = tuple((q, 1) for q in range(8))
AHEAD = 3
DEPTH = GROUP * ROWS
SLAB = GROUP * RING


def remote(src, dst, send_sem, recv_sem, device):
    return pltpu.make_async_remote_copy(
        src_ref=src, dst_ref=dst, send_sem=send_sem, recv_sem=recv_sem,
        device_id=device, device_id_type=MESH)


def kernel(tensor_hbm, tscreen_hbm, density_hbm, dscreen_hbm, out_ref,
           tscreen, dscreen, tb, tf, stage, recv_t, db, dall, perm, dt, part, near, mid, tie, far,
           first, recv_b, tiles, outgoing, fin, ordered,
           load_sem, own_sem, d_send, d_recv, t_send, t_recv,
           near_send, near_recv, mid_send, mid_recv, tie_send, tie_recv, far_send, far_recv,
           b_send, b_recv, f_send, f_recv, hello_a, hello_b, hello_far):
    grid = lax.axis_index("grid")
    z = lax.axis_index("layer")
    core = lax.rem(grid, CORES)
    y = lax.rem(grid // CORES, RING)
    x = grid // (CORES * RING)
    me = x * CORES + core

    def at(x_, y_, core_, z_):
        return ((x_ * RING + y_) * CORES + core_, z_)

    def member(pos):
        return at(pos // CORES, y, lax.rem(pos, CORES), z)

    a = jnp.where(core == 0, y, z)
    b = jnp.where(core == 0, z, y)

    def on_a(i):
        return at(x, jnp.where(core == 0, i, y), core, jnp.where(core == 0, z, i))

    def on_b(i):
        return at(x, jnp.where(core == 0, y, i), core, jnp.where(core == 0, i, z))

    def ring(i):
        return lax.rem(i + 2 * RING, RING)

    def greet(sem, peers):
        for peer in peers:
            pl.semaphore_signal(sem, inc=1, device_id=peer, device_id_type=MESH)

    load_screens = (pltpu.make_async_copy(dscreen_hbm, dscreen, load_sem.at[SLICES]),
                    pltpu.make_async_copy(tscreen_hbm, tscreen, load_sem.at[SLICES + 1]))
    load_d = pltpu.make_async_copy(density_hbm, db, load_sem.at[SLICES + 2])
    load_t = [pltpu.make_async_copy(tensor_hbm.at[:, pl.ds(c * WIDE, WIDE), :], tb.at[c], load_sem.at[c])
              for c in range(SLICES)]
    for copy in (*load_screens, load_d, *load_t):
        copy.start()

    near_a = [on_a(ring(a + 1)), on_a(ring(a - 1))]
    near_b = [on_b(ring(b + 1)), on_b(ring(b - 1))]
    far_b = [on_b(ring(b + 2)), on_b(ring(b - 2))]
    barrier = pltpu.get_barrier_semaphore()
    peers = [member(lax.rem(me + d, GROUP)) for d in range(1, GROUP)] + near_a + near_b
    greet(barrier, peers)

    my_rows = pl.ds(pl.multiple_of(me * ROWS, ROWS), ROWS)
    lane = lax.broadcasted_iota(jnp.int32, (ROWS, LANES), 1)
    load_screens[0].wait()
    load_screens[1].wait()
    load_d.wait()
    for t in range(NSIG // LANES):
        cols = pl.ds(t * LANES, LANES)
        low = dscreen[0, 2 * t].astype(jnp.float32)
        high = dscreen[0, 2 * t + 1].astype(jnp.float32)
        keep = jnp.where(lane < 64, low, high)
        dall[my_rows, cols] = (db[:, cols].astype(jnp.float32) * keep).astype(jnp.bfloat16)

    lane = lax.broadcasted_iota(jnp.int32, (WIDE, LANES), 1)
    keep_t = jnp.where(lane < 64, tscreen[0, 0].astype(jnp.float32), tscreen[0, 1].astype(jnp.float32))

    def regroup(c):
        load_t[c].wait()

        @pl.loop(0, ROWS, unroll=16)
        def _(n):
            tf[c, pl.ds(pl.multiple_of(n * WIDE, WIDE), WIDE), :] = tb[c, n].astype(jnp.float32) * keep_t

        for pos in range(GROUP):
            for h in range(2):
                rows = tf[c, pl.ds(2 * pos + h, ROWS, stride=WIDE), :]
                q = 2 * c + h
                stage[pos, :, q * LANES:(q + 1) * LANES] = rows.astype(jnp.bfloat16)

    regroup(0)
    pl.semaphore_wait(barrier, len(peers))

    other = at(x, y, 1 - core, z)
    d_copies = []
    for d in range(1, NX):
        peer = at(lax.rem(x + d, NX), y, core, z)
        d_copies.append(remote(dall.at[my_rows], dall.at[my_rows], d_send.at[d - 1], d_recv.at[d - 1], peer))
    d_copies.append(remote(dall.at[my_rows], dall.at[my_rows], d_send.at[3], d_recv.at[3], other))
    for copy in d_copies:
        copy.start()

    def span(i):
        q, count = PARTS[i]
        return pl.ds(q * LANES, count * LANES)

    t_copies = {}

    def send_t(i):
        cols = span(i)
        for d in range(1, GROUP):
            pos = lax.rem(me + d, GROUP)
            copy = remote(stage.at[pos, :, cols], recv_t.at[my_rows, cols], t_send.at[i, d - 1],
                          t_recv.at[i, d - 1], member(pos))
            copy.start()
            t_copies[i, d] = copy
        own = pltpu.make_async_copy(stage.at[me, :, cols], recv_t.at[my_rows, cols], own_sem.at[i])
        own.start()
        t_copies[i, 0] = own

    for i in range(2):
        send_t(i)
    greet(hello_a, near_a)
    greet(hello_b, near_b)
    for c in range(1, SLICES):
        regroup(c)

    relays = []
    for d in range(1, NX):
        d_copies[d - 1].wait_recv()
        src = lax.rem(x + NX - d, NX) * CORES + core
        rows = pl.ds(pl.multiple_of(src * ROWS, ROWS), ROWS)
        copy = remote(dall.at[rows], dall.at[rows], d_send.at[3 + d], d_recv.at[3 + d], other)
        copy.start()
        relays.append(copy)
    for i in range(2, AHEAD):
        send_t(i)

    row = lax.broadcasted_iota(jnp.int32, (SLAB, NSIG), 0)
    col = lax.broadcasted_iota(jnp.int32, (SLAB, NSIG), 1)
    j = row & 7
    for block in range(RING):
        y_ = jnp.where(core == 0, block, row >> 3)
        z_ = jnp.where(core == 0, row >> 3, block)
        sigma = (j >> 1) * 128 + y_ * 16 + (j & 1) * 8 + z_
        perm[block * SLAB:(block + 1) * SLAB, :] = jnp.where(sigma == col, 1.0, 0.0).astype(jnp.bfloat16)

    d_copies[3].wait_recv()
    for copy in relays:
        copy.wait_recv()
    dt[...] = lax.dot_general(perm[...], dall[...], (((1,), (1,)), ((), ())),
                              preferred_element_type=jnp.float32).astype(jnp.bfloat16)

    def slab(i, index):
        return part.at[pl.ds(pl.multiple_of(ring(index) * SLAB, SLAB), SLAB), span(i)]

    started = []

    def go(copy):
        copy.start()
        started.append(copy)
        return copy

    near_c, mid_c, tie_c, far_c, b_c = {}, {}, {}, {}, {}

    def multiply(i):
        cols = span(i)
        t_copies[i, 0].wait()
        for d in range(1, GROUP):
            t_copies[i, d].wait_recv()
        if i + AHEAD < len(PARTS):
            send_t(i + AHEAD)
        part[:, cols] = jnp.dot(dt[...], recv_t[:, cols], preferred_element_type=jnp.float32)
        for k, step in enumerate((1, -1)):
            to = on_a(ring(a + step))
            mid_c[i, k] = go(remote(slab(i, a + 3 * step), mid.at[k, :, cols], mid_send.at[i, k],
                                    mid_recv.at[i, k], to))
        if i == 0:
            pl.semaphore_wait(hello_a, 2)
            pl.semaphore_wait(hello_b, 2)
            greet(hello_far, far_b)
        step = -2 if i % 2 == 0 else 2
        tie_c[i] = go(remote(slab(i, a + 4), tie.at[:, cols], tie_send.at[i], tie_recv.at[i],
                             on_a(ring(a + step))))
        for k, step in enumerate((1, -1)):
            to = on_a(ring(a + step))
            near_c[i, k] = go(remote(slab(i, a + step), near.at[k, :, cols], near_send.at[i, k],
                                     near_recv.at[i, k], to))

    def forward(i):
        cols = span(i)
        for k, step in enumerate((2, -2)):
            mid_c[i, k].wait_recv()
            with_tie = k == (1 if i % 2 == 0 else 0)
            if with_tie:
                tie_c[i].wait_recv()
            mine = slab(i, a + step)
            total = mine[...] + mid[k, :, cols]
            if with_tie:
                total = total + tie[:, cols]
            mine[...] = total
            far_c[i, k] = go(remote(mine, far.at[k, :, cols], far_send.at[i, k], far_recv.at[i, k],
                                    on_a(ring(a + step))))

    def reduce_a(i):
        cols = span(i)
        for k in range(2):
            near_c[i, k].wait_recv()
            far_c[i, k].wait_recv()
        first[:, cols] = (slab(i, a)[...] + near[0, :, cols]) + near[1, :, cols] + (far[0, :, cols] + far[1, :, cols])
        if i == 0:
            pl.semaphore_wait(hello_far, 2)
        for d in range(1, RING):
            to = ring(b + d)
            rows = pl.ds(pl.multiple_of(to * GROUP, GROUP), GROUP)
            b_c[i, d] = go(remote(first.at[rows, cols], recv_b.at[d - 1, :, cols], b_send.at[i, d - 1],
                                  b_recv.at[i, d - 1], on_b(to)))

    def reduce_b(i):
        q, count = PARTS[i]
        rows = pl.ds(pl.multiple_of(b * GROUP, GROUP), GROUP)
        total = first[rows, span(i)]
        for d in range(1, RING):
            b_c[i, d].wait_recv()
            total = total + recv_b[d - 1, :, span(i)]
        for h in range(count):
            tiles[(q + h) * GROUP:(q + h + 1) * GROUP, :] = total[:, h * LANES:(h + 1) * LANES]

    last = len(PARTS)
    for step in range(last + 6):
        if step < last:
            multiply(step)
        if 0 <= step - 2 < last:
            forward(step - 2)
        if 0 <= step - 4 < last:
            reduce_a(step - 4)
        if 0 <= step - 6 < last:
            reduce_b(step - 6)

    for k in range(GROUP):
        outgoing[k] = tiles[pl.ds(k, 8, stride=GROUP), :]
    mine = pl.ds(pl.multiple_of(me * 8, 8), 8)
    f_c = []
    for d in range(1, GROUP):
        pos = lax.rem(me + d, GROUP)
        copy = remote(outgoing.at[pos], fin.at[mine], f_send.at[d - 1], f_recv.at[d - 1], member(pos))
        copy.start()
        f_c.append(copy)
    fin[mine, :] = outgoing[me]
    for copy in d_copies + relays + started:
        copy.wait_send()
    for i in range(last):
        for d in range(1, GROUP):
            t_copies[i, d].wait_send()
    for copy in f_c:
        copy.wait()
    for q in range(8):
        ordered[pl.ds(WIDE * (q // 2) + q % 2, GROUP, stride=2), :] = fin[pl.ds(q, GROUP, stride=8), :]
    out_ref[...] = ordered[...].astype(jnp.bfloat16)


def body(tensor_blocks, tensor_screen, density, density_screen):
    dma = pltpu.SemaphoreType.DMA
    regular = pltpu.SemaphoreType.REGULAR
    parts = len(PARTS)
    out = pl.pallas_call(
        kernel,
        out_shape=jax.ShapeDtypeStruct((NAUX, LANES), jnp.bfloat16),
        in_specs=[pl.BlockSpec(memory_space=pltpu.HBM)] * 4,
        out_specs=pl.BlockSpec(memory_space=pltpu.VMEM),
        scratch_shapes=[
            pltpu.SMEM((1, 2), jnp.int32),
            pltpu.SMEM((1, 8), jnp.int32),
            pltpu.VMEM((SLICES, ROWS, WIDE, LANES), jnp.bfloat16),
            pltpu.VMEM((SLICES, ROWS * WIDE, LANES), jnp.float32),
            pltpu.VMEM((GROUP, ROWS, SHARE), jnp.bfloat16),
            pltpu.VMEM((DEPTH, SHARE), jnp.bfloat16),
            pltpu.VMEM((ROWS, NSIG), jnp.bfloat16),
            pltpu.VMEM((DEPTH, NSIG), jnp.bfloat16),
            pltpu.VMEM((NSIG, NSIG), jnp.bfloat16),
            pltpu.VMEM((NSIG, DEPTH), jnp.bfloat16),
            pltpu.VMEM((NSIG, SHARE), jnp.float32),
            pltpu.VMEM((2, SLAB, SHARE), jnp.float32),
            pltpu.VMEM((2, SLAB, SHARE), jnp.float32),
            pltpu.VMEM((SLAB, SHARE), jnp.float32),
            pltpu.VMEM((2, SLAB, SHARE), jnp.float32),
            pltpu.VMEM((SLAB, SHARE), jnp.float32),
            pltpu.VMEM((RING - 1, GROUP, SHARE), jnp.float32),
            pltpu.VMEM((8 * GROUP, LANES), jnp.float32),
            pltpu.VMEM((GROUP, 8, LANES), jnp.float32),
            pltpu.VMEM((NAUX, LANES), jnp.float32),
            pltpu.VMEM((NAUX, LANES), jnp.float32),
            dma((SLICES + 3,)), dma((parts,)),
            dma((7,)), dma((7,)),
            dma((parts, 7)), dma((parts, 7)),
            dma((parts, 2)), dma((parts, 2)),
            dma((parts, 2)), dma((parts, 2)),
            dma((parts,)), dma((parts,)),
            dma((parts, 2)), dma((parts, 2)),
            dma((parts, 7)), dma((parts, 7)),
            dma((7,)), dma((7,)),
            regular, regular, regular,
        ],
        compiler_params=pltpu.CompilerParams(
            collective_id=0, has_side_effects=True, vmem_limit_bytes=40 << 20),
        name="contract",
    )(*(pltpu.with_memory_space_constraint(v, pltpu.HBM)
        for v in (tensor_blocks, tensor_screen, density, density_screen)))
    return out.reshape(1, NAUX, LANES)


def solution(mesh):
    in_specs = (
        P(("grid", "layer"), None, None),
        P(("grid", "layer"), None),
        P(("grid", "layer"), None),
        P(("grid", "layer"), None),
    )
    out_specs = P(("grid", "layer"), None, None)
    return jax.shard_map(body, mesh=mesh, in_specs=in_specs, out_specs=out_specs, check_vma=False)
```

time: 59.5 us -> 56.9 us (0.956)
  local copies, waits for them, and re-layouts: 3.98 us -> 0.61 us
  Pallas kernels: 55.3 us -> 56.1 us
    unnamed x9 -> x1, local copies, waits for them, and re-layouts: 3.98 us -> 0.61 us
    pallas_call x1, Pallas kernels: 55.3 us -> 56.1 us  [body(): pl.pallas_call(kernel, out_shape=jax.ShapeDtypeStruct((NAUX, LANES), jnp....]
where the time goes in v2:
time: 56.9 us; the launch traced here: 56.7 us
  Pallas kernels  56.1 us (99%)
  local copies, waits for them, and re-layouts  0.61 us (1%)
    pallas_call x1, Pallas kernels, body(): pl.pallas_call(kernel, out_shape=jax.ShapeDtypeStruct((NAUX, LANES), jnp....  56.1 us

profile of v2, /device:TPU:1, one launch (start us, length us, event | category | flops | bytes accessed | tf_op | source)
XLA Modules:
  0.0 56.7 jit_solution(2325983981467215688)
XLA Ops:
  0.0 56.1 %contract.1 = bf16[64,128]{1,0:T(8,128)(2,1)S(1)} custom-call(bf16[64,64,128]{2,1,0:T(8,128)(2,1)} %tensor_hbm.1, s32[1,2]{1,0:T(1,128)} %tscreen_hbm.1, bf16[64,512]{1,0:T(8,128)(2,1)} %density_hbm.1, s32[1,8]{1,0:T(1,128)} %dscreen_hbm.1), custom_call_target="tpu_custom_call" | custom-call | tf_op jit(solution)/shard_map/contract/pallas_call | solution.py:284
  56.1 0.6 %copy.6 = bf16[1,64,128]{2,1,0:T(8,128)(2,1)} copy(bf16[1,64,128]{2,1,0:T(8,128)(2,1)S(1)} %bitcast.1) | data formatting | bytes 32768

commit v3 on v2

--- a/solution.py
+++ b/solution.py
@@ -17,7 +17,9 @@
 WIDE = NAUX // SLICES
 SHARE = NAUX // GROUP * LANES
 PARTS = tuple((q, 1) for q in range(8))
-AHEAD = 3
+STEPS = 32000.0
+TINY = 1e-33
+AHEAD = 4
 DEPTH = GROUP * ROWS
 SLAB = GROUP * RING
 
@@ -29,10 +31,10 @@
 
 
 def kernel(tensor_hbm, tscreen_hbm, density_hbm, dscreen_hbm, out_ref,
-           tscreen, dscreen, tb, tf, stage, recv_t, db, dall, perm, dt, part, near, mid, tie, far,
+           tscreen, dscreen, tb, tf, stage, recv_t, db, dall, perm, dt, part, coded, unit, near, units,
            first, recv_b, tiles, outgoing, fin, ordered,
            load_sem, own_sem, d_send, d_recv, t_send, t_recv,
-           near_send, near_recv, mid_send, mid_recv, tie_send, tie_recv, far_send, far_recv,
+           near_send, near_recv, unit_send, unit_recv,
            b_send, b_recv, f_send, f_recv, hello_a, hello_b, hello_far):
     grid = lax.axis_index("grid")
     z = lax.axis_index("layer")
@@ -73,6 +75,7 @@
 
     near_a = [on_a(ring(a + 1)), on_a(ring(a - 1))]
     near_b = [on_b(ring(b + 1)), on_b(ring(b - 1))]
+    far_a = [on_a(ring(a + 2)), on_a(ring(a - 2))]
     far_b = [on_b(ring(b + 2)), on_b(ring(b - 2))]
     barrier = pltpu.get_barrier_semaphore()
     peers = [member(lax.rem(me + d, GROUP)) for d in range(1, GROUP)] + near_a + near_b
@@ -169,8 +172,8 @@
     dt[...] = lax.dot_general(perm[...], dall[...], (((1,), (1,)), ((), ())),
                               preferred_element_type=jnp.float32).astype(jnp.bfloat16)
 
-    def slab(i, index):
-        return part.at[pl.ds(pl.multiple_of(ring(index) * SLAB, SLAB), SLAB), span(i)]
+    def slab(ref, i, index):
+        return ref.at[pl.ds(pl.multiple_of(ring(index) * SLAB, SLAB), SLAB), span(i)]
 
     started = []
 
@@ -179,7 +182,7 @@
         started.append(copy)
         return copy
 
-    near_c, mid_c, tie_c, far_c, b_c = {}, {}, {}, {}, {}
+    near_c, unit_c, b_c = {}, {}, {}
 
     def multiply(i):
         cols = span(i)
@@ -188,46 +191,30 @@
             t_copies[i, d].wait_recv()
         if i + AHEAD < len(PARTS):
             send_t(i + AHEAD)
-        part[:, cols] = jnp.dot(dt[...], recv_t[:, cols], preferred_element_type=jnp.float32)
-        for k, step in enumerate((1, -1)):
-            to = on_a(ring(a + step))
-            mid_c[i, k] = go(remote(slab(i, a + 3 * step), mid.at[k, :, cols], mid_send.at[i, k],
-                                    mid_recv.at[i, k], to))
+        sums = jnp.dot(dt[...], recv_t[:, cols], preferred_element_type=jnp.float32)
+        part[:, cols] = sums
+        largest = jnp.maximum(jnp.max(jnp.abs(sums), axis=0, keepdims=True), TINY)
+        unit[i] = largest * (1.0 / STEPS)
+        coded[:, cols] = jnp.round(sums * (STEPS / largest)).astype(jnp.int32).astype(jnp.int16)
         if i == 0:
             pl.semaphore_wait(hello_a, 2)
             pl.semaphore_wait(hello_b, 2)
-            greet(hello_far, far_b)
-        step = -2 if i % 2 == 0 else 2
-        tie_c[i] = go(remote(slab(i, a + 4), tie.at[:, cols], tie_send.at[i], tie_recv.at[i],
-                             on_a(ring(a + step))))
-        for k, step in enumerate((1, -1)):
-            to = on_a(ring(a + step))
-            near_c[i, k] = go(remote(slab(i, a + step), near.at[k, :, cols], near_send.at[i, k],
-                                     near_recv.at[i, k], to))
-
-    def forward(i):
-        cols = span(i)
-        for k, step in enumerate((2, -2)):
-            mid_c[i, k].wait_recv()
-            with_tie = k == (1 if i % 2 == 0 else 0)
-            if with_tie:
-                tie_c[i].wait_recv()
-            mine = slab(i, a + step)
-            total = mine[...] + mid[k, :, cols]
-            if with_tie:
-                total = total + tie[:, cols]
-            mine[...] = total
-            far_c[i, k] = go(remote(mine, far.at[k, :, cols], far_send.at[i, k], far_recv.at[i, k],
-                                    on_a(ring(a + step))))
+            greet(hello_far, far_b + far_a)
+            pl.semaphore_wait(hello_far, 4)
+        for d in (4, 3, 5, 2, 6, 1, 7):
+            unit_c[i, d] = go(remote(unit.at[i], units.at[d - 1, i], unit_send.at[i, d - 1],
+                                     unit_recv.at[i, d - 1], on_a(ring(a + d))))
+            near_c[i, d] = go(remote(slab(coded, i, a + d), near.at[d - 1, :, cols], near_send.at[i, d - 1],
+                                     near_recv.at[i, d - 1], on_a(ring(a + d))))
 
     def reduce_a(i):
         cols = span(i)
-        for k in range(2):
-            near_c[i, k].wait_recv()
-            far_c[i, k].wait_recv()
-        first[:, cols] = (slab(i, a)[...] + near[0, :, cols]) + near[1, :, cols] + (far[0, :, cols] + far[1, :, cols])
-        if i == 0:
-            pl.semaphore_wait(hello_far, 2)
+        total = slab(part, i, a)[...]
+        for d in range(1, RING):
+            near_c[i, d].wait_recv()
+            unit_c[i, d].wait_recv()
+            total = total + near[d - 1, :, cols].astype(jnp.int32).astype(jnp.float32) * units[d - 1, i]
+        first[:, cols] = total
         for d in range(1, RING):
             to = ring(b + d)
             rows = pl.ds(pl.multiple_of(to * GROUP, GROUP), GROUP)
@@ -245,15 +232,13 @@
             tiles[(q + h) * GROUP:(q + h + 1) * GROUP, :] = total[:, h * LANES:(h + 1) * LANES]
 
     last = len(PARTS)
-    for step in range(last + 6):
+    for step in range(last + 8):
         if step < last:
             multiply(step)
-        if 0 <= step - 2 < last:
-            forward(step - 2)
         if 0 <= step - 4 < last:
             reduce_a(step - 4)
-        if 0 <= step - 6 < last:
-            reduce_b(step - 6)
+        if 0 <= step - 8 < last:
+            reduce_b(step - 8)
 
     for k in range(GROUP):
         outgoing[k] = tiles[pl.ds(k, 8, stride=GROUP), :]
@@ -298,10 +283,10 @@
             pltpu.VMEM((NSIG, NSIG), jnp.bfloat16),
             pltpu.VMEM((NSIG, DEPTH), jnp.bfloat16),
             pltpu.VMEM((NSIG, SHARE), jnp.float32),
-            pltpu.VMEM((2, SLAB, SHARE), jnp.float32),
-            pltpu.VMEM((2, SLAB, SHARE), jnp.float32),
-            pltpu.VMEM((SLAB, SHARE), jnp.float32),
-            pltpu.VMEM((2, SLAB, SHARE), jnp.float32),
+            pltpu.VMEM((NSIG, SHARE), jnp.int16),
+            pltpu.VMEM((parts, 1, LANES), jnp.float32),
+            pltpu.VMEM((RING - 1, SLAB, SHARE), jnp.int16),
+            pltpu.VMEM((RING - 1, parts, 1, LANES), jnp.float32),
             pltpu.VMEM((SLAB, SHARE), jnp.float32),
             pltpu.VMEM((RING - 1, GROUP, SHARE), jnp.float32),
             pltpu.VMEM((8 * GROUP, LANES), jnp.float32),
@@ -311,10 +296,8 @@
             dma((SLICES + 3,)), dma((parts,)),
             dma((7,)), dma((7,)),
             dma((parts, 7)), dma((parts, 7)),
-            dma((parts, 2)), dma((parts, 2)),
-            dma((parts, 2)), dma((parts, 2)),
-            dma((parts,)), dma((parts,)),
-            dma((parts, 2)), dma((parts, 2)),
+            dma((parts, 7)), dma((parts, 7)),
+            dma((parts, 7)), dma((parts, 7)),
             dma((parts, 7)), dma((parts, 7)),
             dma((7,)), dma((7,)),
             regular, regular, regular,

time: 56.9 us -> 53.3 us (0.937)
  Pallas kernels: 56.1 us -> 52.5 us
    pallas_call x1, Pallas kernels: 56.1 us -> 52.5 us  [body(): pl.pallas_call(kernel, out_shape=jax.ShapeDtypeStruct((NAUX, LANES), jnp....]
where the time goes in v3:
time: 53.3 us; the launch traced here: 53.1 us
  Pallas kernels  52.5 us (98%)
  local copies, waits for them, and re-layouts  0.61 us (1%)
    pallas_call x1, Pallas kernels, body(): pl.pallas_call(kernel, out_shape=jax.ShapeDtypeStruct((NAUX, LANES), jnp....  52.5 us

profile of v3, /device:TPU:1, one launch (start us, length us, event | category | flops | bytes accessed | tf_op | source)
XLA Modules:
  0.0 53.1 jit_solution(9421882593308233746)
XLA Ops:
  0.0 52.5 %contract.1 = bf16[64,128]{1,0:T(8,128)(2,1)S(1)} custom-call(bf16[64,64,128]{2,1,0:T(8,128)(2,1)} %tensor_hbm.1, s32[1,2]{1,0:T(1,128)} %tscreen_hbm.1, bf16[64,512]{1,0:T(8,128)(2,1)} %density_hbm.1, s32[1,8]{1,0:T(1,128)} %dscreen_hbm.1), custom_call_target="tpu_custom_call" | custom-call | tf_op jit(solution)/shard_map/contract/pallas_call | solution.py:269
  52.5 0.6 %copy.6 = bf16[1,64,128]{2,1,0:T(8,128)(2,1)} copy(bf16[1,64,128]{2,1,0:T(8,128)(2,1)S(1)} %bitcast.1) | data formatting | bytes 32768

commit v4 on v3

--- a/solution.py
+++ b/solution.py
@@ -15,11 +15,11 @@
 NSIG = 512
 SLICES = 4
 WIDE = NAUX // SLICES
-SHARE = NAUX // GROUP * LANES
-PARTS = tuple((q, 1) for q in range(8))
+PARTS = 4
+WIDTH = 2 * LANES
 STEPS = 32000.0
 TINY = 1e-33
-AHEAD = 4
+AHEAD = 2
 DEPTH = GROUP * ROWS
 SLAB = GROUP * RING
 
@@ -106,10 +106,8 @@
         for pos in range(GROUP):
             for h in range(2):
                 rows = tf[c, pl.ds(2 * pos + h, ROWS, stride=WIDE), :]
-                q = 2 * c + h
-                stage[pos, :, q * LANES:(q + 1) * LANES] = rows.astype(jnp.bfloat16)
-
-    regroup(0)
+                stage[c, pos, :, h * LANES:(h + 1) * LANES] = rows.astype(jnp.bfloat16)
+
     pl.semaphore_wait(barrier, len(peers))
 
     other = at(x, y, 1 - core, z)
@@ -121,25 +119,21 @@
     for copy in d_copies:
         copy.start()
 
-    def span(i):
-        q, count = PARTS[i]
-        return pl.ds(q * LANES, count * LANES)
-
     t_copies = {}
 
     def send_t(i):
-        cols = span(i)
         for d in range(1, GROUP):
             pos = lax.rem(me + d, GROUP)
-            copy = remote(stage.at[pos, :, cols], recv_t.at[my_rows, cols], t_send.at[i, d - 1],
-                          t_recv.at[i, d - 1], member(pos))
+            copy = remote(stage.at[i, pos], recv_t.at[i, my_rows], t_send.at[i, d - 1], t_recv.at[i, d - 1],
+                          member(pos))
             copy.start()
             t_copies[i, d] = copy
-        own = pltpu.make_async_copy(stage.at[me, :, cols], recv_t.at[my_rows, cols], own_sem.at[i])
+        own = pltpu.make_async_copy(stage.at[i, me], recv_t.at[i, my_rows], own_sem.at[i])
         own.start()
         t_copies[i, 0] = own
 
-    for i in range(2):
+    regroup(0)
+    for i in range(1):
         send_t(i)
     greet(hello_a, near_a)
     greet(hello_b, near_b)
@@ -154,7 +148,7 @@
         copy = remote(dall.at[rows], dall.at[rows], d_send.at[3 + d], d_recv.at[3 + d], other)
         copy.start()
         relays.append(copy)
-    for i in range(2, AHEAD):
+    for i in range(1, AHEAD):
         send_t(i)
 
     row = lax.broadcasted_iota(jnp.int32, (SLAB, NSIG), 0)
@@ -173,7 +167,7 @@
                               preferred_element_type=jnp.float32).astype(jnp.bfloat16)
 
     def slab(ref, i, index):
-        return ref.at[pl.ds(pl.multiple_of(ring(index) * SLAB, SLAB), SLAB), span(i)]
+        return ref.at[i, pl.ds(pl.multiple_of(ring(index) * SLAB, SLAB), SLAB)]
 
     started = []
 
@@ -185,17 +179,16 @@
     near_c, unit_c, b_c = {}, {}, {}
 
     def multiply(i):
-        cols = span(i)
         t_copies[i, 0].wait()
         for d in range(1, GROUP):
             t_copies[i, d].wait_recv()
-        if i + AHEAD < len(PARTS):
+        if i + AHEAD < PARTS:
             send_t(i + AHEAD)
-        sums = jnp.dot(dt[...], recv_t[:, cols], preferred_element_type=jnp.float32)
-        part[:, cols] = sums
+        sums = jnp.dot(dt[...], recv_t[i], preferred_element_type=jnp.float32)
+        part[i] = sums
         largest = jnp.maximum(jnp.max(jnp.abs(sums), axis=0, keepdims=True), TINY)
         unit[i] = largest * (1.0 / STEPS)
-        coded[:, cols] = jnp.round(sums * (STEPS / largest)).astype(jnp.int32).astype(jnp.int16)
+        coded[i] = jnp.round(sums * (STEPS / largest)).astype(jnp.int32).astype(jnp.int16)
         if i == 0:
             pl.semaphore_wait(hello_a, 2)
             pl.semaphore_wait(hello_b, 2)
@@ -204,41 +197,40 @@
         for d in (4, 3, 5, 2, 6, 1, 7):
             unit_c[i, d] = go(remote(unit.at[i], units.at[d - 1, i], unit_send.at[i, d - 1],
                                      unit_recv.at[i, d - 1], on_a(ring(a + d))))
-            near_c[i, d] = go(remote(slab(coded, i, a + d), near.at[d - 1, :, cols], near_send.at[i, d - 1],
+            near_c[i, d] = go(remote(slab(coded, i, a + d), near.at[d - 1, i], near_send.at[i, d - 1],
                                      near_recv.at[i, d - 1], on_a(ring(a + d))))
 
     def reduce_a(i):
-        cols = span(i)
         total = slab(part, i, a)[...]
         for d in range(1, RING):
             near_c[i, d].wait_recv()
             unit_c[i, d].wait_recv()
-            total = total + near[d - 1, :, cols].astype(jnp.int32).astype(jnp.float32) * units[d - 1, i]
-        first[:, cols] = total
+            total = total + near[d - 1, i].astype(jnp.int32).astype(jnp.float32) * units[d - 1, i]
+        first[i] = total
         for d in range(1, RING):
             to = ring(b + d)
             rows = pl.ds(pl.multiple_of(to * GROUP, GROUP), GROUP)
-            b_c[i, d] = go(remote(first.at[rows, cols], recv_b.at[d - 1, :, cols], b_send.at[i, d - 1],
+            b_c[i, d] = go(remote(first.at[i, rows], recv_b.at[d - 1, i], b_send.at[i, d - 1],
                                   b_recv.at[i, d - 1], on_b(to)))
 
     def reduce_b(i):
-        q, count = PARTS[i]
         rows = pl.ds(pl.multiple_of(b * GROUP, GROUP), GROUP)
-        total = first[rows, span(i)]
+        total = first[i, rows, :]
         for d in range(1, RING):
             b_c[i, d].wait_recv()
-            total = total + recv_b[d - 1, :, span(i)]
-        for h in range(count):
-            tiles[(q + h) * GROUP:(q + h + 1) * GROUP, :] = total[:, h * LANES:(h + 1) * LANES]
-
-    last = len(PARTS)
-    for step in range(last + 8):
+            total = total + recv_b[d - 1, i]
+        for h in range(2):
+            q = 2 * i + h
+            tiles[q * GROUP:(q + 1) * GROUP, :] = total[:, h * LANES:(h + 1) * LANES]
+
+    last = PARTS
+    for step in range(last + 4):
         if step < last:
             multiply(step)
+        if 0 <= step - 2 < last:
+            reduce_a(step - 2)
         if 0 <= step - 4 < last:
-            reduce_a(step - 4)
-        if 0 <= step - 8 < last:
-            reduce_b(step - 8)
+            reduce_b(step - 4)
 
     for k in range(GROUP):
         outgoing[k] = tiles[pl.ds(k, 8, stride=GROUP), :]
@@ -265,7 +257,7 @@
 def body(tensor_blocks, tensor_screen, density, density_screen):
     dma = pltpu.SemaphoreType.DMA
     regular = pltpu.SemaphoreType.REGULAR
-    parts = len(PARTS)
+    parts = PARTS
     out = pl.pallas_call(
         kernel,
         out_shape=jax.ShapeDtypeStruct((NAUX, LANES), jnp.bfloat16),
@@ -276,19 +268,19 @@
             pltpu.SMEM((1, 8), jnp.int32),
             pltpu.VMEM((SLICES, ROWS, WIDE, LANES), jnp.bfloat16),
             pltpu.VMEM((SLICES, ROWS * WIDE, LANES), jnp.float32),
-            pltpu.VMEM((GROUP, ROWS, SHARE), jnp.bfloat16),
-            pltpu.VMEM((DEPTH, SHARE), jnp.bfloat16),
+            pltpu.VMEM((parts, GROUP, ROWS, WIDTH), jnp.bfloat16),
+            pltpu.VMEM((parts, DEPTH, WIDTH), jnp.bfloat16),
             pltpu.VMEM((ROWS, NSIG), jnp.bfloat16),
             pltpu.VMEM((DEPTH, NSIG), jnp.bfloat16),
             pltpu.VMEM((NSIG, NSIG), jnp.bfloat16),
             pltpu.VMEM((NSIG, DEPTH), jnp.bfloat16),
-            pltpu.VMEM((NSIG, SHARE), jnp.float32),
-            pltpu.VMEM((NSIG, SHARE), jnp.int16),
-            pltpu.VMEM((parts, 1, LANES), jnp.float32),
-            pltpu.VMEM((RING - 1, SLAB, SHARE), jnp.int16),
-            pltpu.VMEM((RING - 1, parts, 1, LANES), jnp.float32),
-            pltpu.VMEM((SLAB, SHARE), jnp.float32),
-            pltpu.VMEM((RING - 1, GROUP, SHARE), jnp.float32),
+            pltpu.VMEM((parts, NSIG, WIDTH), jnp.float32),
+            pltpu.VMEM((parts, NSIG, WIDTH), jnp.int16),
+            pltpu.VMEM((parts, 1, WIDTH), jnp.float32),
+            pltpu.VMEM((RING - 1, parts, SLAB, WIDTH), jnp.int16),
+            pltpu.VMEM((RING - 1, parts, 1, WIDTH), jnp.float32),
+            pltpu.VMEM((parts, SLAB, WIDTH), jnp.float32),
+            pltpu.VMEM((RING - 1, parts, GROUP, WIDTH), jnp.float32),
             pltpu.VMEM((8 * GROUP, LANES), jnp.float32),
             pltpu.VMEM((GROUP, 8, LANES), jnp.float32),
             pltpu.VMEM((NAUX, LANES), jnp.float32),

time: 53.3 us -> 52.5 us (0.985)
  Pallas kernels: 52.5 us -> 51.7 us
    pallas_call x1, Pallas kernels: 52.5 us -> 51.7 us  [body(): pl.pallas_call(kernel, out_shape=jax.ShapeDtypeStruct((NAUX, LANES), jnp....]
where the time goes in v4:
time: 52.5 us; the launch traced here: 52.3 us
  Pallas kernels  51.7 us (98%)
  local copies, waits for them, and re-layouts  0.61 us (1%)
    pallas_call x1, Pallas kernels, body(): pl.pallas_call(kernel, out_shape=jax.ShapeDtypeStruct((NAUX, LANES), jnp....  51.7 us

profile of v4, /device:TPU:1, one launch (start us, length us, event | category | flops | bytes accessed | tf_op | source)
XLA Modules:
  0.0 52.3 jit_solution(951190689587957402)
XLA Ops:
  0.0 51.7 %contract.1 = bf16[64,128]{1,0:T(8,128)(2,1)S(1)} custom-call(bf16[64,64,128]{2,1,0:T(8,128)(2,1)} %tensor_hbm.1, s32[1,2]{1,0:T(1,128)} %tscreen_hbm.1, bf16[64,512]{1,0:T(8,128)(2,1)} %density_hbm.1, s32[1,8]{1,0:T(1,128)} %dscreen_hbm.1), custom_call_target="tpu_custom_call" | custom-call | tf_op jit(solution)/shard_map/contract/pallas_call | solution.py:261
  51.7 0.6 %copy.6 = bf16[1,64,128]{2,1,0:T(8,128)(2,1)} copy(bf16[1,64,128]{2,1,0:T(8,128)(2,1)S(1)} %bitcast.1) | data formatting | bytes 32768
